TPU v7x, 32 devices: a whole 2x2x4 slice. The times are simulated.
32 devices in a mesh: fsdp: 16 (over z, x, core), seq: 2 (over y).
Axes of the slice: x: 2, y: 2, z: 4, core: 2. Of those that a mesh axis runs over, the one named last changes fastest.
Arguments:
- latents: float32 [32, 128, 768], P('fsdp', 'seq'), may hold values from -6 to 6
- cond_pick: int32 [32], P('fsdp'), may hold values from 0 to 999
- cond_table: float32 [1000, 768], replicated, may hold values from -6 to 6
- w_ada: bfloat16 [2, 768, 4608], P(None, None, ('fsdp', 'seq')), may hold values from -0.21875 to 0.21875
- b_ada: bfloat16 [2, 4608], P(None, ('fsdp', 'seq')), may hold values from -3 to 3
- w_qkv: bfloat16 [2, 768, 2304], P(None, None, ('fsdp', 'seq')), may hold values from -0.21875 to 0.21875
- w_out: bfloat16 [2, 768, 768], P(None, None, ('fsdp', 'seq')), may hold values from -1.5 to 1.5
- w_up: bfloat16 [2, 768, 3072], P(None, None, ('fsdp', 'seq')), may hold values from -0.21875 to 0.21875
- w_down: bfloat16 [2, 3072, 768], P(None, ('fsdp', 'seq')), may hold values from -0.109375 to 0.109375
- cotangent: float32 [32, 128, 768], P('fsdp', 'seq'), may hold values from -6 to 6
Outputs:
- output: float32 [32, 128, 768], P('fsdp', 'seq')
- grad_latents: float32 [32, 128, 768], P('fsdp', 'seq')
- grad_table: float32 [1000, 768], P(None, ('fsdp', 'seq'))
- grad_w_ada: float32 [2, 768, 4608], P(None, None, ('fsdp', 'seq'))
- grad_b_ada: float32 [2, 4608], P(None, ('fsdp', 'seq'))
- grad_w_qkv: float32 [2, 768, 2304], P(None, None, ('fsdp', 'seq'))
- grad_w_out: float32 [2, 768, 768], P(None, None, ('fsdp', 'seq'))
- grad_w_up: float32 [2, 768, 3072], P(None, None, ('fsdp', 'seq'))
- grad_w_down: float32 [2, 3072, 768], P(None, ('fsdp', 'seq'))
Inputs may be any that keep to these rules, and one draw needn't show every extreme that they name: `cond_pick`: each latent's row of cond_table.
All inputs are finite; a program needn't handle non-finite values.
Results may differ from a plain program's by a relative error of at most 0.023.
Values may be sent and summed in bfloat16 or wider, within the bound.
A program may use at most 320 MiB of HBM per device.

v0:
```python
import jax
import jax.numpy as jnp
from jax import lax
from jax.sharding import PartitionSpec as P

HEADS = 12
MB = 2


EPS = 1e-06
HIGH = lax.Precision.HIGHEST


def norm_rows(values):
    centred = values - jnp.mean(values, -1, keepdims=True)
    inverse = lax.rsqrt(jnp.mean(centred * centred, -1, keepdims=True) + EPS)
    return (centred * inverse, inverse)


def norm_back(normed, inverse, grad_in):
    return inverse * (
        grad_in
        - jnp.mean(grad_in, -1, keepdims=True)
        - normed * jnp.mean(grad_in * normed, -1, keepdims=True)
    )


def gelu_tanh(values):
    return jax.nn.gelu(values, approximate=True)


def split_heads(rows, head_count):
    return rows.reshape(rows.shape[0], rows.shape[1], head_count, rows.shape[2] // head_count)


def layer_forward(stream, condition, weights, head_count):
    w_ada, b_ada, w_qkv, w_out, w_up, w_down = weights
    model_width = stream.shape[-1]
    head_size = model_width // head_count
    modulation = jnp.dot(
        condition, w_ada, precision=HIGH, preferred_element_type=jnp.float32
    ) + b_ada.astype(jnp.float32)
    pieces = [
        modulation[:, None, piece_index * model_width : (piece_index + 1) * model_width]
        for piece_index in range(6)
    ]
    normed, inverse = norm_rows(stream)
    hidden_in = (normed * (1.0 + pieces[1]) + pieces[0]).astype(jnp.bfloat16)
    qkv_rows = jnp.einsum(
        "btd,de->bte", hidden_in, w_qkv, preferred_element_type=jnp.float32
    ).astype(jnp.bfloat16)
    key_rows, value_rows = (
        lax.all_gather(qkv_rows[..., model_width : 2 * model_width], "seq", axis=1, tiled=True),
        lax.all_gather(qkv_rows[..., 2 * model_width :], "seq", axis=1, tiled=True),
    )
    scores = jnp.einsum(
        "bqhd,bkhd->bhqk",
        split_heads(qkv_rows[..., :model_width], head_count),
        split_heads(key_rows, head_count),
        preferred_element_type=jnp.float32,
    ) * head_size ** (-0.5)
    row_max = jnp.max(scores, -1, keepdims=True)
    exp_scores = jnp.exp(scores - row_max)
    row_sum = jnp.sum(exp_scores, -1, keepdims=True)
    soft_probs = (exp_scores / row_sum).astype(jnp.bfloat16)
    log_total = row_max + jnp.log(row_sum)
    attn_mixed = (
        jnp.einsum(
            "bhqk,bkhd->bqhd",
            soft_probs,
            split_heads(value_rows, head_count),
            preferred_element_type=jnp.float32,
        )
        .reshape(stream.shape)
        .astype(jnp.bfloat16)
    )
    branch = jnp.einsum("btd,de->bte", attn_mixed, w_out, preferred_element_type=jnp.float32)
    middle = stream + pieces[2] * branch
    normed_mlp, inverse_mlp = norm_rows(middle)
    hidden_mlp = (normed_mlp * (1.0 + pieces[4]) + pieces[3]).astype(jnp.bfloat16)
    mlp_upper = jnp.einsum("btd,df->btf", hidden_mlp, w_up, preferred_element_type=jnp.float32)
    active = gelu_tanh(mlp_upper).astype(jnp.bfloat16)
    mlp_down = jnp.einsum("btf,fd->btd", active, w_down, preferred_element_type=jnp.float32)
    saved = (
        pieces,
        normed,
        inverse,
        hidden_in,
        qkv_rows,
        log_total,
        attn_mixed,
        branch,
        normed_mlp,
        inverse_mlp,
        hidden_mlp,
        mlp_upper,
        active,
        mlp_down,
    )
    return (middle + pieces[5] * mlp_down, saved)


def layer_backward(saved, condition, weights, grad_out, head_count):
    w_ada, b_ada, w_qkv, w_out, w_up, w_down = weights
    (
        pieces,
        normed,
        inverse,
        hidden_in,
        qkv_rows,
        log_total,
        attn_mixed,
        branch,
        normed_mlp,
        inverse_mlp,
        hidden_mlp,
        mlp_upper,
        active,
        mlp_down,
    ) = saved
    model_width = grad_out.shape[-1]
    scale_factor = (model_width // head_count) ** (-0.5)
    grad_gate_mlp = jnp.sum(grad_out * mlp_down, 1)
    grad_down = (pieces[5] * grad_out).astype(jnp.bfloat16)
    weight_down = jnp.einsum("btd,btf->df", grad_down, active, preferred_element_type=jnp.float32)
    grad_active = jnp.einsum("btd,fd->btf", grad_down, w_down, preferred_element_type=jnp.float32)
    _, gelu_pull = jax.vjp(gelu_tanh, mlp_upper)
    grad_upper = gelu_pull(grad_active)[0].astype(jnp.bfloat16)
    weight_up = jnp.einsum(
        "btd,btf->df", hidden_mlp, grad_upper, preferred_element_type=jnp.float32
    )
    grad_hidden_mlp = jnp.einsum(
        "btf,df->btd", grad_upper, w_up, preferred_element_type=jnp.float32
    )
    grad_shift_mlp = jnp.sum(grad_hidden_mlp, 1)
    grad_scale_mlp = jnp.sum(grad_hidden_mlp * normed_mlp, 1)
    grad_middle = grad_out + norm_back(normed_mlp, inverse_mlp, grad_hidden_mlp * (1.0 + pieces[4]))
    grad_gate_attn = jnp.sum(grad_middle * branch, 1)
    grad_branch = (pieces[2] * grad_middle).astype(jnp.bfloat16)
    weight_out = jnp.einsum(
        "btd,bte->de", attn_mixed, grad_branch, preferred_element_type=jnp.float32
    )
    grad_mixed = jnp.einsum(
        "bte,de->btd", grad_branch, w_out, preferred_element_type=jnp.float32
    ).astype(jnp.bfloat16)
    key_rows, value_rows = (
        lax.all_gather(qkv_rows[..., model_width : 2 * model_width], "seq", axis=1, tiled=True),
        lax.all_gather(qkv_rows[..., 2 * model_width :], "seq", axis=1, tiled=True),
    )
    query_heads = split_heads(qkv_rows[..., :model_width], head_count)
    key_heads = split_heads(key_rows, head_count)
    value_heads = split_heads(value_rows, head_count)
    scores = (
        jnp.einsum("bqhd,bkhd->bhqk", query_heads, key_heads, preferred_element_type=jnp.float32)
        * scale_factor
    )
    soft_full = jnp.exp(scores - log_total)
    soft_probs = soft_full.astype(jnp.bfloat16)
    mixed_heads = split_heads(grad_mixed, head_count)
    grad_probs = jnp.einsum(
        "bqhd,bkhd->bhqk", mixed_heads, value_heads, preferred_element_type=jnp.float32
    )
    grad_values = jnp.einsum(
        "bhqk,bqhd->bkhd", soft_probs, mixed_heads, preferred_element_type=jnp.float32
    ).reshape(key_rows.shape)
    inner = jnp.sum(grad_probs * soft_full, -1, keepdims=True)
    grad_scores = (soft_full * (grad_probs - inner)).astype(jnp.bfloat16)
    grad_queries = (
        jnp.einsum(
            "bhqk,bkhd->bqhd", grad_scores, key_heads, preferred_element_type=jnp.float32
        ).reshape(grad_out.shape)
        * scale_factor
    )
    grad_keys = (
        jnp.einsum(
            "bhqk,bqhd->bkhd", grad_scores, query_heads, preferred_element_type=jnp.float32
        ).reshape(key_rows.shape)
        * scale_factor
    )
    grad_keys, grad_values = (
        lax.psum_scatter(
            grad_keys.astype(jnp.bfloat16), "seq", scatter_dimension=1, tiled=True
        ).astype(jnp.float32),
        lax.psum_scatter(
            grad_values.astype(jnp.bfloat16), "seq", scatter_dimension=1, tiled=True
        ).astype(jnp.float32),
    )
    grad_qkv = jnp.concatenate([grad_queries, grad_keys, grad_values], -1).astype(jnp.bfloat16)
    weight_qkv = jnp.einsum("btd,bte->de", hidden_in, grad_qkv, preferred_element_type=jnp.float32)
    grad_hidden = jnp.einsum("bte,de->btd", grad_qkv, w_qkv, preferred_element_type=jnp.float32)
    grad_shift_attn = jnp.sum(grad_hidden, 1)
    grad_scale_attn = jnp.sum(grad_hidden * normed, 1)
    grad_stream = grad_middle + norm_back(normed, inverse, grad_hidden * (1.0 + pieces[1]))
    grad_mod = jnp.concatenate(
        [
            grad_shift_attn,
            grad_scale_attn,
            grad_gate_attn,
            grad_shift_mlp,
            grad_scale_mlp,
            grad_gate_mlp,
        ],
        -1,
    )
    weight_ada = jnp.dot(condition.T, grad_mod, precision=HIGH, preferred_element_type=jnp.float32)
    bias_ada = jnp.sum(grad_mod, 0)
    grad_condition = jnp.einsum(
        "be,de->bd", grad_mod, w_ada, precision=HIGH, preferred_element_type=jnp.float32
    )
    return (
        grad_stream,
        (weight_ada, bias_ada, weight_qkv, weight_out, weight_up, weight_down),
        grad_condition,
        grad_mod,
    )


def local(latents, cond_pick, cond_table, w_ada, b_ada, w_qkv, w_out, w_up, w_down, cotangent):
    layers = w_ada.shape[0]
    local_latents = latents.shape[0]
    per_batch = local_latents // MB
    table_rows = cond_table.shape[0]
    one_hot = (cond_pick[:, None] == jnp.arange(table_rows, dtype=jnp.int32)[None, :]).astype(
        jnp.float32
    )
    condition_all = jnp.dot(one_hot, cond_table, precision=HIGH, preferred_element_type=jnp.float32)
    silu_all, silu_pull = jax.vjp(jax.nn.silu, condition_all)
    totals = [None] * layers
    mod_lists = [[] for layer_index in range(layers)]
    outputs = []
    grad_inputs = []
    grad_conditions = []
    for micro_index in range(MB):
        first_row = micro_index * per_batch
        stream = latents[first_row : first_row + per_batch]
        condition = silu_all[first_row : first_row + per_batch]
        saved_list = []
        for layer_index in range(layers):
            weights = (
                lax.all_gather(w_ada[layer_index], ("fsdp", "seq"), axis=1, tiled=True),
                lax.all_gather(b_ada[layer_index], ("fsdp", "seq"), axis=0, tiled=True),
                lax.all_gather(w_qkv[layer_index], ("fsdp", "seq"), axis=1, tiled=True),
                lax.all_gather(w_out[layer_index], ("fsdp", "seq"), axis=1, tiled=True),
                lax.all_gather(w_up[layer_index], ("fsdp", "seq"), axis=1, tiled=True),
                lax.all_gather(w_down[layer_index], ("fsdp", "seq"), axis=0, tiled=True),
            )
            stream, saved = layer_forward(stream, condition, weights, HEADS)
            saved_list.append(saved)
        outputs.append(stream)
        grad_stream = cotangent[first_row : first_row + per_batch]
        grad_condition = jnp.zeros_like(condition)
        for layer_index in reversed(range(layers)):
            weights = (
                lax.all_gather(w_ada[layer_index], ("fsdp", "seq"), axis=1, tiled=True),
                lax.all_gather(b_ada[layer_index], ("fsdp", "seq"), axis=0, tiled=True),
                lax.all_gather(w_qkv[layer_index], ("fsdp", "seq"), axis=1, tiled=True),
                lax.all_gather(w_out[layer_index], ("fsdp", "seq"), axis=1, tiled=True),
                lax.all_gather(w_up[layer_index], ("fsdp", "seq"), axis=1, tiled=True),
                lax.all_gather(w_down[layer_index], ("fsdp", "seq"), axis=0, tiled=True),
            )
            grad_stream, layer_grads, grad_part, grad_mod = layer_backward(
                saved_list[layer_index], condition, weights, grad_stream, HEADS
            )
            grad_condition = grad_condition + grad_part
            mod_lists[layer_index].append(grad_mod)
            if totals[layer_index] is None:
                totals[layer_index] = layer_grads
            else:
                totals[layer_index] = tuple(
                    (earlier + latest for earlier, latest in zip(totals[layer_index], layer_grads))
                )
        grad_inputs.append(grad_stream)
        grad_conditions.append(grad_condition)
    grad_cond_rows = jnp.concatenate(grad_conditions, 0)
    stacked = [
        jnp.stack([totals[layer_index][member] for layer_index in range(layers)])
        for member in range(6)
    ]
    grad_cond = silu_pull(grad_cond_rows)[0]
    grad_table = jnp.dot(one_hot.T, grad_cond, precision=HIGH, preferred_element_type=jnp.float32)
    summed = (
        lax.psum_scatter(stacked[0], ("fsdp", "seq"), scatter_dimension=2, tiled=True),
        lax.psum_scatter(stacked[1], ("fsdp", "seq"), scatter_dimension=1, tiled=True),
        lax.psum_scatter(stacked[2], ("fsdp", "seq"), scatter_dimension=2, tiled=True),
        lax.psum_scatter(stacked[3], ("fsdp", "seq"), scatter_dimension=2, tiled=True),
        lax.psum_scatter(stacked[4], ("fsdp", "seq"), scatter_dimension=2, tiled=True),
        lax.psum_scatter(stacked[5], ("fsdp", "seq"), scatter_dimension=2, tiled=True),
        lax.psum_scatter(grad_table, ("fsdp", "seq"), scatter_dimension=1, tiled=True),
    )
    return (
        jnp.concatenate(outputs, 0),
        jnp.concatenate(grad_inputs, 0),
        summed[6],
        summed[0],
        summed[1],
        summed[2],
        summed[3],
        summed[4],
        jnp.swapaxes(summed[5], 1, 2),
    )


def solution(mesh):
    placed = (
        P("fsdp", "seq", None),
        P("fsdp"),
        P(),
        P(None, None, ("fsdp", "seq")),
        P(None, ("fsdp", "seq")),
        P(None, None, ("fsdp", "seq")),
        P(None, None, ("fsdp", "seq")),
        P(None, None, ("fsdp", "seq")),
        P(None, ("fsdp", "seq"), None),
        P("fsdp", "seq", None),
    )
    return jax.shard_map(
        local,
        mesh=mesh,
        in_specs=placed,
        out_specs=(
            P("fsdp", "seq", None),
            P("fsdp", "seq", None),
            P(None, ("fsdp", "seq")),
            P(None, None, ("fsdp", "seq")),
            P(None, ("fsdp", "seq")),
            P(None, None, ("fsdp", "seq")),
            P(None, None, ("fsdp", "seq")),
            P(None, None, ("fsdp", "seq")),
            P(None, ("fsdp", "seq"), None),
        ),
        check_vma=False,
    )
```

profile of v0, /device:TPU:0, one launch (start us, length us, event | category | flops | bytes accessed | tf_op | source)
XLA Modules:
  0.0 2294.2 jit_solution(2049913889021249706)
XLA Ops:
  22.4 43.0 %all-reduce.7 = (bf16[4608]{0:T(1024)(128)(2,1)S(1)}, bf16[4608]{0:T(1024)(128)(2,1)S(1)}) all-reduce(bf16[4608]{0:T(1024)(128)(2,1)S(1)} %dynamic-update-slice, bf16[4608]{0:T(1024)(128)(2,1)S(1)} %dynamic-update-slice.1), channel_id=3, replica_groups=mesh['fsdp'=16,'seq'=2] {'fsdp','seq'}, use_global_device_ids=true, to_apply=%add | all-reduce | flops 9216 | bytes 36864
  67.2 20.1 all-gather.23.cloned.1.call-done
  87.3 8.7 fusion.127
  96.0 5.6 fusion.124
  101.7 60.6 %all-gather.33.cloned.1.call-done = bf16[1,768,4608]{1,2,0:T(8,128)(2,1)} async-done(((bf16[1,768,144]{1,2,0:T(8,128)(2,1)}), bf16[1,768,4608]{1,2,0:T(8,128)(2,1)}) %all-gather.33.cloned.1.call-update) | async-done | bytes 7077904 | tf_op jit(solution)/shard_map/all_gather | solution.py:240
  162.3 8.7 fusion.133
  171.0 5.6 fusion.130
  176.8 47.2 %all-gather.25.cloned.1.call-done = bf16[1,768,2304]{1,2,0:T(8,128)(2,1)} async-done(((bf16[1,768,72]{1,2,0:T(8,128)(2,1)}), bf16[1,768,2304]{1,2,0:T(8,128)(2,1)}) %all-gather.25.cloned.1.call-update) | async-done | bytes 3538960 | tf_op jit(solution)/shard_map/all_gather | solution.py:242
  224.0 3.2 fusion.82
  227.2 5.6 all_gather.57
  233.2 5.8 all_gather.56
  239.3 3.2 fusion.85
  242.6 5.3 all_gather.44
  248.2 5.8 all_gather.43
  256.7 23.0 %all-gather.27.cloned.1.call-done = bf16[1,768,768]{1,2,0:T(8,128)(2,1)} async-done(((bf16[1,768,24]{1,2,0:T(8,128)(2,1)}), bf16[1,768,768]{1,2,0:T(8,128)(2,1)}) %all-gather.27.cloned.1.call-update) | async-done | bytes 1179664 | tf_op jit(solution)/shard_map/all_gather | solution.py:243
  284.9 60.8 %all-gather.29.cloned.1.call-done = bf16[1,768,3072]{1,2,0:T(8,128)(2,1)} async-done(((bf16[1,768,96]{1,2,0:T(8,128)(2,1)}), bf16[1,768,3072]{1,2,0:T(8,128)(2,1)}) %all-gather.29.cloned.1.call-update) | async-done | bytes 4718608 | tf_op jit(solution)/shard_map/all_gather | solution.py:244
  345.6 3.9 fusion.44
  349.6 61.9 %all-gather.31.cloned.1.call-done = bf16[1,3072,768]{2,1,0:T(8,128)(2,1)} async-done(((bf16[1,96,768]{2,1,0:T(8,128)(2,1)}), bf16[1,3072,768]{2,1,0:T(8,128)(2,1)}) %all-gather.31.cloned.1.call-update) | async-done | bytes 4718608 | tf_op jit(solution)/shard_map/all_gather | solution.py:245
  411.5 4.1 fusion.363
  415.9 58.1 %all-gather.35.cloned.1.call-done = bf16[1,768,2304]{1,2,0:T(8,128)(2,1)} async-done(((bf16[1,768,72]{1,2,0:T(8,128)(2,1)}), bf16[1,768,2304]{1,2,0:T(8,128)(2,1)}) %all-gather.35.cloned.1.call-update) | async-done | bytes 3538960 | tf_op jit(solution)/shard_map/all_gather | solution.py:242
  474.0 3.2 fusion.76
  477.3 5.6 all_gather.59
  483.3 5.7 all_gather.58
  490.3 40.1 %all-gather.37.cloned.1.call-done = bf16[1,768,768]{1,2,0:T(8,128)(2,1)} async-done(((bf16[1,768,24]{1,2,0:T(8,128)(2,1)}), bf16[1,768,768]{1,2,0:T(8,128)(2,1)}) %all-gather.37.cloned.1.call-update) | async-done | bytes 1179664 | tf_op jit(solution)/shard_map/all_gather | solution.py:243
  533.3 63.3 %all-gather.39.cloned.1.call-done = bf16[1,768,3072]{1,2,0:T(8,128)(2,1)} async-done(((bf16[1,768,96]{1,2,0:T(8,128)(2,1)}), bf16[1,768,3072]{1,2,0:T(8,128)(2,1)}) %all-gather.39.cloned.1.call-update) | async-done | bytes 4718608 | tf_op jit(solution)/shard_map/all_gather | solution.py:244
  596.6 3.9 fusion.28
  600.5 61.9 %all-gather.41.cloned.1.call-done = bf16[1,3072,768]{2,1,0:T(8,128)(2,1)} async-done(((bf16[1,96,768]{2,1,0:T(8,128)(2,1)}), bf16[1,3072,768]{2,1,0:T(8,128)(2,1)}) %all-gather.41.cloned.1.call-update) | async-done | bytes 4718608 | tf_op jit(solution)/shard_map/all_gather | solution.py:245
  662.4 4.2 fusion.175
  678.4 4.0 fusion.46
  682.5 4.4 fusion.360
  688.4 5.6 all_gather.52
  695.6 5.5 all_gather.51
  706.0 4.4 fusion.30
  710.5 4.3 fusion.161
  735.2 6.3 fusion.283
  741.6 8.8 add_bitcast_fusion.2
  753.5 9.3 reduce-scatter.34.cloned.1.call-done
  764.7 11.8 reduce-scatter.36.cloned.1.call-done
  785.7 4.0 fusion.168
  822.7 6.1 fusion.275
  829.1 8.9 add_bitcast_fusion.3
  841.5 11.9 reduce-scatter.38.cloned.1.call-done
  854.5 12.4 reduce-scatter.40.cloned.1.call-done
  868.3 3.3 fusion.350
  871.6 3.4 fusion.209
  878.8 13.0 pad_maximum_fusion.2
  891.8 28.4 %copy.110 = f32[2,768,3072]{1,0,2:T(2,128)} copy(f32[2,768,3072]{2,1,0:T(8,128)} %pad_maximum_fusion.2) | data formatting | bytes 37748736 | tf_op jit(solution)/shard_map/stack | solution.py:276
  928.3 6.8 pad_maximum_fusion.1
  935.1 28.3 %copy.109 = f32[2,768,3072]{1,0,2:T(2,128)} copy(f32[2,768,3072]{2,1,0:T(8,128)} %pad_maximum_fusion.1) | data formatting | bytes 37748736 | tf_op jit(solution)/shard_map/stack | solution.py:276
  969.6 8.3 copy.108
  979.3 4.1 add_bitcast_fusion.6
  984.6 4.2 add_bitcast_fusion.7
  988.8 12.0 pad_maximum_fusion.3
  1000.9 21.7 copy.107
  1022.9 5.2 fusion.142
  1028.1 5.3 fusion.145
  1033.4 5.4 fusion.136
  1045.1 3.5 add_bitcast_fusion.1
  1048.6 9.8 pad_maximum_fusion
  1064.2 223.2 %all-reduce.14.cloned.1.call-done = f32[2,768,3072]{1,0,2:T(2,128)} async-done(((f32[2,768,3072]{1,0,2:T(2,128)}), f32[2,768,3072]{1,0,2:T(2,128)}) %all-reduce.14.cloned.1.call-update) | async-done | bytes 18874384
  1289.4 308.6 %all-reduce.12.cloned.1.call-done = f32[2,768,3072]{1,0,2:T(2,128)} async-done(((f32[2,768,3072]{1,0,2:T(2,128)}), f32[2,768,3072]{1,0,2:T(2,128)}) %all-reduce.12.cloned.1.call-update) | async-done | bytes 18874384
  1600.0 309.7 %all-reduce.16.cloned.1.call-done = (f32[2,768,2304]{1,0,2:T(2,128)}, f32[2,768,768]{1,0,2:T(2,128)}) async-done(((f32[2,768,2304]{1,0,2:T(2,128)}, f32[2,768,768]{1,0,2:T(2,128)}), (f32[2,768,2304]{1,0,2:T(2,128)}, f32[2,768,768]{1,0,2:T(2,128)})) %all-reduce.16.cloned.1.call-update) | async-done | bytes 18874384
  1913.1 104.9 %reduce-scatter.30.cloned.1.call-done = f32[1000,24]{0,1:T(8,128)} async-done(((f32[1000,768]{0,1:T(8,128)}), f32[1000,24]{0,1:T(8,128)}) %reduce-scatter.30.cloned.1.call-update) | async-done | bytes 96016 | tf_op jit(solution)/shard_map/reduce_scatter | solution.py:288
  2018.0 269.1 %reduce-scatter.32.cloned.1.call-done = f32[2,768,144]{1,2,0:T(8,128)} async-done(((f32[2,768,4608]{1,2,0:T(8,128)}), f32[2,768,144]{1,2,0:T(8,128)}) %reduce-scatter.32.cloned.1.call-update) | async-done | bytes 884752 | tf_op jit(solution)/shard_map/reduce_scatter | solution.py:282
  (683 shorter events, 162.2 us)
Async XLA Ops:
  7.2 58.3 %copy-start = (f32[1000,768]{1,0:T(8,128)S(1)}, f32[1000,768]{1,0:T(8,128)}, u32[]{:S(2)}) copy-start(f32[1000,768]{1,0:T(8,128)} %param.12) | copy-start | bytes 9216004
  7.2 58.3 %copy-start.178 = (s32[2]{0:T(128)S(1)}, s32[2]{0:T(128)}, u32[]{:S(2)}) copy-start(s32[2]{0:T(128)} %param.11) | copy-start | bytes 28
  7.2 80.0 %all-gather.23.cloned.1.call-start = ((), (), s32[]{:S(2)}) async-start(), calls=%async_computation.13 | async-start | bytes 7299072 | tf_op jit(solution)/shard_map/all_gather | solution.py:240
  9.3 153.0 %all-gather.33.cloned.1.call-start = ((), (), s32[]{:S(2)}) async-start(), calls=%async_computation.18 | async-start | bytes 7299072 | tf_op jit(solution)/shard_map/all_gather | solution.py:240
  10.1 213.9 %all-gather.25.cloned.1.call-start = ((), (), s32[]{:S(2)}) async-start(), calls=%async_computation.14 | async-start | bytes 3649536 | tf_op jit(solution)/shard_map/all_gather | solution.py:242
  11.8 267.9 %all-gather.27.cloned.1.call-start = ((), (), s32[]{:S(2)}) async-start(), calls=%async_computation.15 | async-start | bytes 1216512 | tf_op jit(solution)/shard_map/all_gather | solution.py:243
  13.3 332.4 %all-gather.29.cloned.1.call-start = ((), (), s32[]{:S(2)}) async-start(), calls=%async_computation.16 | async-start | bytes 4866048 | tf_op jit(solution)/shard_map/all_gather | solution.py:244
  15.1 396.4 %all-gather.31.cloned.1.call-start = ((), (), s32[]{:S(2)}) async-start(), calls=%async_computation.17 | async-start | bytes 4866048 | tf_op jit(solution)/shard_map/all_gather | solution.py:245
  16.8 457.2 %all-gather.35.cloned.1.call-start = ((), (), s32[]{:S(2)}) async-start(), calls=%async_computation.19 | async-start | bytes 3649536 | tf_op jit(solution)/shard_map/all_gather | solution.py:242
  17.6 512.9 %all-gather.37.cloned.1.call-start = ((), (), s32[]{:S(2)}) async-start(), calls=%async_computation.20 | async-start | bytes 1216512 | tf_op jit(solution)/shard_map/all_gather | solution.py:243
  18.3 578.2 %all-gather.39.cloned.1.call-start = ((), (), s32[]{:S(2)}) async-start(), calls=%async_computation.21 | async-start | bytes 4866048 | tf_op jit(solution)/shard_map/all_gather | solution.py:244
  19.1 643.3 %all-gather.41.cloned.1.call-start = ((), (), s32[]{:S(2)}) async-start(), calls=%async_computation.22 | async-start | bytes 4866048 | tf_op jit(solution)/shard_map/all_gather | solution.py:245
  19.7 731.3 %reduce-scatter.42.cloned.1.call-start = ((), (), s32[]{:S(2)}) async-start(), calls=%async_computation.27 | async-start | bytes 294912
  21.6 217.6 %copy-start.114 = (f32[64]{0:T(128)}, f32[64]{0:T(128)S(1)}, u32[]{:S(2)}) copy-start(f32[64]{0:T(128)S(1)} %broadcast_multiply_fusion.23) | copy-start | bytes 772
  21.7 202.3 %copy-start.141 = (f32[64]{0:T(128)}, f32[64]{0:T(128)S(1)}, u32[]{:S(2)}) copy-start(f32[64]{0:T(128)S(1)} %broadcast_multiply_fusion.19) | copy-start | bytes 772
  21.9 217.4 %copy-start.153 = (f32[64]{0:T(128)}, f32[64]{0:T(128)S(1)}, u32[]{:S(2)}) copy-start(f32[64]{0:T(128)S(1)} %add_rsqrt_fusion.7) | copy-start | bytes 772
  21.9 202.0 %copy-start.166 = (f32[64]{0:T(128)}, f32[64]{0:T(128)S(1)}, u32[]{:S(2)}) copy-start(f32[64]{0:T(128)S(1)} %add_rsqrt_fusion.3) | copy-start | bytes 772
  67.2 103.8 %copy-start.87 = (f32[2,768]{1,0:T(2,128)}, f32[2,768]{1,0:T(2,128)S(1)}, u32[]{:S(2)}) copy-start(f32[2,768]{1,0:T(2,128)S(1)} %get-tuple-element.174) | copy-start | bytes 18436
  176.7 62.3 %copy-start.101 = (f32[768]{0:T(1024)}, f32[768]{0:T(1024)S(1)}, u32[]{:S(2)}) copy-start(f32[768]{0:T(1024)S(1)} %get-tuple-element.97) | copy-start | bytes 9220
  176.7 168.9 %copy-start.103 = (f32[768]{0:T(1024)}, f32[768]{0:T(1024)S(1)}, u32[]{:S(2)}) copy-start(f32[768]{0:T(1024)S(1)} %get-tuple-element.95) | copy-start | bytes 9220
  176.7 620.9 %copy-start.97 = (f32[768]{0:T(1024)}, f32[768]{0:T(1024)S(1)}, u32[]{:S(2)}) copy-start(f32[768]{0:T(1024)S(1)} %get-tuple-element.99) | copy-start | bytes 9220
  239.3 569.8 %copy-start.93 = (f32[768]{0:T(1024)}, f32[768]{0:T(1024)S(1)}, u32[]{:S(2)}) copy-start(f32[768]{0:T(1024)S(1)} %get-tuple-element.87) | copy-start | bytes 9220
  254.2 219.8 %copy-start.105 = (f32[768]{0:T(1024)}, f32[768]{0:T(1024)S(1)}, u32[]{:S(2)}) copy-start(f32[768]{0:T(1024)S(1)} %get-tuple-element.91) | copy-start | bytes 9220
  254.2 342.4 %copy-start.107 = (f32[768]{0:T(1024)}, f32[768]{0:T(1024)S(1)}, u32[]{:S(2)}) copy-start(f32[768]{0:T(1024)S(1)} %get-tuple-element.89) | copy-start | bytes 9220
  254.2 416.5 %copy-start.99 = (f32[768]{0:T(1024)}, f32[768]{0:T(1024)S(1)}, u32[]{:S(2)}) copy-start(f32[768]{0:T(1024)S(1)} %get-tuple-element.93) | copy-start | bytes 9220
  255.0 94.6 %copy-start.111 = (f32[12,64]{1,0:T(8,128)}, f32[12,64]{1,0:T(8,128)S(1)}, u32[]{:S(2)}) copy-start(f32[12,64]{1,0:T(8,128)S(1)} %fusion.184) | copy-start | bytes 9220
  255.7 93.8 %copy-start.109 = (f32[12,64]{1,0:T(8,128)}, f32[12,64]{1,0:T(8,128)S(1)}, u32[]{:S(2)}) copy-start(f32[12,64]{1,0:T(8,128)S(1)} %fusion.186) | copy-start | bytes 9220
  256.2 93.3 %copy-start.82 = (bf16[12,64,64]{2,1,0:T(8,128)(2,1)}, bf16[12,64,64]{2,1,0:T(8,128)(2,1)S(1)}, u32[]{:S(2)}) copy-start(bf16[12,64,64]{2,1,0:T(8,128)(2,1)S(1)} %convolution_convert_fusion.7) | copy-start | bytes 294916
  256.7 92.9 %copy-start.72 = (bf16[12,64,64]{2,1,0:T(8,128)(2,1)}, bf16[12,64,64]{2,1,0:T(8,128)(2,1)S(1)}, u32[]{:S(2)}) copy-start(bf16[12,64,64]{2,1,0:T(8,128)(2,1)S(1)} %convolution_convert_fusion.5) | copy-start | bytes 294916
  281.5 130.0 %copy-start.48 = (f32[64,768]{1,0:T(8,128)}, f32[64,768]{1,0:T(8,128)S(1)}, u32[]{:S(2)}) copy-start(f32[64,768]{1,0:T(8,128)S(1)} %fusion.100) | copy-start | bytes 589828
  284.7 130.9 %copy-start.145 = (f32[64]{0:T(128)}, f32[64]{0:T(128)S(1)}, u32[]{:S(2)}) copy-start(f32[64]{0:T(128)S(1)} %broadcast_multiply_fusion.18) | copy-start | bytes 772
  284.9 130.8 %copy-start.170 = (f32[64]{0:T(128)}, f32[64]{0:T(128)S(1)}, u32[]{:S(2)}) copy-start(f32[64]{0:T(128)S(1)} %add_rsqrt_fusion.2) | copy-start | bytes 772
  349.6 127.7 %copy-start.17 = (f32[64,3072]{1,0:T(8,128)}, f32[64,3072]{1,0:T(8,128)S(1)}, u32[]{:S(2)}) copy-start(f32[64,3072]{1,0:T(8,128)S(1)} %fusion.44) | copy-start | bytes 2359300
  415.6 114.9 %copy-start.9 = (f32[1,64,768]{2,1,0:T(8,128)}, f32[1,64,768]{2,1,0:T(8,128)S(1)}, u32[]{:S(2)}) copy-start(f32[1,64,768]{2,1,0:T(8,128)S(1)} %get-tuple-element.129) | copy-start | bytes 589828
  415.6 74.7 %copy-start.150 = (f32[64]{0:T(128)}, f32[64]{0:T(128)S(1)}, u32[]{:S(2)}) copy-start(f32[64]{0:T(128)S(1)} %broadcast_multiply_fusion.17) | copy-start | bytes 772
  415.9 73.3 %copy-start.175 = (f32[64]{0:T(128)}, f32[64]{0:T(128)S(1)}, u32[]{:S(2)}) copy-start(f32[64]{0:T(128)S(1)} %add_rsqrt_fusion.1) | copy-start | bytes 772
  483.1 47.4 %copy-start.56 = (bf16[1,128,768]{1,2,0:T(8,128)(2,1)}, bf16[1,128,768]{1,2,0:T(8,128)(2,1)S(1)}, u32[]{:S(2)}) copy-start(bf16[1,128,768]{1,2,0:T(8,128)(2,1)S(1)} %copy.93) | copy-start | bytes 589828
  483.3 113.3 %copy-start.57 = (bf16[1,64,768]{1,2,0:T(8,128)(2,1)}, bf16[1,64,768]{1,2,0:T(8,128)(2,1)S(1)}, u32[]{:S(2)}) copy-start(bf16[1,64,768]{1,2,0:T(8,128)(2,1)S(1)} %copy.144) | copy-start | bytes 294916
  489.1 107.5 %copy-start.80 = (bf16[1,128,768]{1,2,0:T(8,128)(2,1)}, bf16[1,128,768]{1,2,0:T(8,128)(2,1)S(1)}, u32[]{:S(2)}) copy-start(bf16[1,128,768]{1,2,0:T(8,128)(2,1)S(1)} %copy.92) | copy-start | bytes 589828
  490.3 106.3 %copy-start.74 = (bf16[12,64,64]{2,1,0:T(8,128)(2,1)}, bf16[12,64,64]{2,1,0:T(8,128)(2,1)S(1)}, u32[]{:S(2)}) copy-start(bf16[12,64,64]{2,1,0:T(8,128)(2,1)S(1)} %convolution_convert_fusion.4) | copy-start | bytes 294916
  533.0 129.4 %copy-start.11 = (f32[1,64,768]{2,1,0:T(8,128)}, f32[1,64,768]{2,1,0:T(8,128)S(1)}, u32[]{:S(2)}) copy-start(f32[1,64,768]{2,1,0:T(8,128)S(1)} %get-tuple-element.127) | copy-start | bytes 589828
  533.1 136.9 %copy-start.148 = (f32[64]{0:T(128)}, f32[64]{0:T(128)S(1)}, u32[]{:S(2)}) copy-start(f32[64]{0:T(128)S(1)} %broadcast_multiply_fusion.16) | copy-start | bytes 772
  533.3 136.7 %copy-start.173 = (f32[64]{0:T(128)}, f32[64]{0:T(128)S(1)}, u32[]{:S(2)}) copy-start(f32[64]{0:T(128)S(1)} %add_rsqrt_fusion) | copy-start | bytes 772
  600.5 61.9 %copy-start.20 = (f32[64,3072]{1,0:T(8,128)}, f32[64,3072]{1,0:T(8,128)S(1)}, u32[]{:S(2)}) copy-start(f32[64,3072]{1,0:T(8,128)S(1)} %fusion.28) | copy-start | bytes 2359300
  678.2 42.3 %copy-start.95 = (f32[768]{0:T(1024)}, f32[768]{0:T(1024)S(1)}, u32[]{:S(2)}) copy-start(f32[768]{0:T(1024)S(1)} %get-tuple-element.81) | copy-start | bytes 9220
  726.6 25.6 %reduce-scatter.44.cloned.1.call-start = ((), (), s32[]{:S(2)}) async-start(), calls=%async_computation.28 | async-start | bytes 294912
  735.2 27.7 %reduce-scatter.34.cloned.1.call-start = ((), (), s32[]{:S(2)}) async-start(), calls=%async_computation.23 | async-start | bytes 294912
  741.5 36.8 %copy-start.123 = (f32[64]{0:T(128)S(1)}, f32[64]{0:T(128)}, u32[]{:S(2)}) copy-start(f32[64]{0:T(128)} %copy-done.122) | copy-start | bytes 772
  741.5 36.8 %copy-start.164 = (f32[64]{0:T(128)S(1)}, f32[64]{0:T(128)}, u32[]{:S(2)}) copy-start(f32[64]{0:T(128)} %copy-done.163) | copy-start | bytes 772
  741.6 34.9 %reduce-scatter.36.cloned.1.call-start = ((), (), s32[]{:S(2)}) async-start(), calls=%async_computation.24 | async-start | bytes 294912
  750.5 87.8 %reduce-scatter.46.cloned.1.call-start = ((), (), s32[]{:S(2)}) async-start(), calls=%async_computation.29 | async-start | bytes 294912
  815.5 24.8 %reduce-scatter.48.cloned.1.call-start = ((), (), s32[]{:S(2)}) async-start(), calls=%async_computation.30 | async-start | bytes 294912
  822.6 30.7 %reduce-scatter.38.cloned.1.call-start = ((), (), s32[]{:S(2)}) async-start(), calls=%async_computation.25 | async-start | bytes 294912
  828.9 39.4 %copy-start.37 = (bf16[12,64,64]{2,1,0:T(8,128)(2,1)S(1)}, bf16[12,64,64]{2,1,0:T(8,128)(2,1)}, u32[]{:S(2)}) copy-start(bf16[12,64,64]{2,1,0:T(8,128)(2,1)} %fusion.110) | copy-start | bytes 294916
  828.9 38.1 %reduce-scatter.40.cloned.1.call-start = ((), (), s32[]{:S(2)}) async-start(), calls=%async_computation.26 | async-start | bytes 294912
  838.0 33.5 %copy-start.154 = (f32[64]{0:T(128)S(1)}, f32[64]{0:T(128)}, u32[]{:S(2)}) copy-start(f32[64]{0:T(128)} %copy-done.153) | copy-start | bytes 772
  838.0 33.5 %copy-start.167 = (f32[64]{0:T(128)S(1)}, f32[64]{0:T(128)}, u32[]{:S(2)}) copy-start(f32[64]{0:T(128)} %copy-done.166) | copy-start | bytes 772
  838.1 224.6 %reduce-scatter.50.cloned.1.call-start = ((), (), s32[]{:S(2)}) async-start(), calls=%async_computation.31 | async-start | bytes 2433024
  878.8 408.6 %all-reduce.14.cloned.1.call-start = ((), (), s32[]{:S(2)}) async-start(), calls=%async_computation.33 | async-start | bytes 37748736
  920.2 677.7 %all-reduce.12.cloned.1.call-start = ((), (), s32[]{:S(2)}) async-start(), calls=%async_computation.32 | async-start | bytes 37748736
  963.5 946.1 %all-reduce.16.cloned.1.call-start = ((), (), s32[]{:S(2)}) async-start(), calls=%async_computation.34 | async-start | bytes 37748736
  1022.6 995.5 %reduce-scatter.30.cloned.1.call-start = ((), (), s32[]{:S(2)}) async-start(), calls=%async_computation.11 | async-start | bytes 3244032 | tf_op jit(solution)/shard_map/reduce_scatter | solution.py:288
  1045.0 1242.1 %reduce-scatter.32.cloned.1.call-start = ((), (), s32[]{:S(2)}) async-start(), calls=%async_computation.12 | async-start | bytes 29196288 | tf_op jit(solution)/shard_map/reduce_scatter | solution.py:282
  1060.2 1226.9 %copy-start.1 = (f32[1000,768]{1,0:T(8,128)S(1)}, f32[1000,768]{1,0:T(8,128)}, u32[]{:S(2)}) copy-start(f32[1000,768]{1,0:T(8,128)} %param.12) | copy-start | bytes 9216004
  (155 other events, 1195.5 us)
Sparse Core Ops, SparseCore 0:
  11.5 75.6 all-gather.22
  90.7 71.4 all-gather.32
  165.2 58.7 all-gather.24
  226.7 52.9 all-gather.26
  283.0 62.5 all-gather.28
  349.0 62.4 all-gather.30
  415.0 58.9 all-gather.34
  477.5 52.9 all-gather.36
  534.0 62.5 all-gather.38
  599.9 62.4 all-gather.40
  726.7 9.7 reduce-scatter.41
  738.6 10.9 reduce-scatter.43
  751.8 10.9 reduce-scatter.33
  765.5 10.9 reduce-scatter.35
  815.6 10.9 reduce-scatter.45
  829.3 10.9 reduce-scatter.47
  842.3 10.9 reduce-scatter.37
  856.0 10.9 reduce-scatter.39
  878.9 98.9 reduce-scatter.49
  984.9 302.4 all-reduce.13
  1294.6 303.3 all-reduce.11
  1605.5 304.0 all-reduce.15
  1916.5 101.4 reduce-scatter.29
  2026.0 261.0 reduce-scatter.31
where the time goes:
time: 2300 us; the launch traced here: 2290 us
  waiting for transfers between devices  1760 us (77%)
  matrix products  212 us (9%)
  local copies, waits for them, and re-layouts  144 us (6%)
  blocking collectives  88 us (4%)
  other arithmetic  67.5 us (3%)
    unnamed x36, waiting for transfers between devices  891 us
    reduce_scatter x1, waiting for transfers between devices, local(): lax.psum_scatter(stacked[0], ('fsdp', 'seq'), scatter_dimension=2, tiled=...  269 us
    all_gather x2, waiting for transfers between devices, local(): lax.all_gather(w_up[layer_index], ('fsdp', 'seq'), axis=1, tiled=True)  124 us
    all_gather x2, waiting for transfers between devices, local(): lax.all_gather(w_down[layer_index], ('fsdp', 'seq'), axis=0, tiled=True)  124 us
    all_gather x2, waiting for transfers between devices, local(): lax.all_gather(w_qkv[layer_index], ('fsdp', 'seq'), axis=1, tiled=True)  105 us
    reduce_scatter x1, waiting for transfers between devices, local(): lax.psum_scatter(grad_table, ('fsdp', 'seq'), scatter_dimension=1, tiled=...  105 us
    another operation x4, local copies, waits for them, and re-layouts, local(): jnp.stack([totals[layer_index][member] for layer_index in range(layers)])  86.6 us
    all_gather x2, waiting for transfers between devices, local(): lax.all_gather(w_ada[layer_index], ('fsdp', 'seq'), axis=1, tiled=True)  80.7 us
  transfers between devices with their start and end apart: 24, of which 20 were waited for; matrix products, arithmetic and copies ran while one was open for 14% of the time, Pallas kernels for 0%

commit v1 on v0

v1 whole, which is shorter than its diff:
```python
import functools

import jax
import jax.numpy as jnp
from jax import lax
from jax.experimental import pallas as pl
from jax.experimental.pallas import tpu as pltpu
from jax.sharding import PartitionSpec as P

HEADS = 12
EPS = 1e-06
HIGH = lax.Precision.HIGHEST
BOTH = ("fsdp", "seq")
MESH = pl.DeviceIdType.MESH


def exchange_kernel(fsdp_size, seq_size, x_ref, y_ref, send_sem, recv_sem, local_sem):
    count = fsdp_size * seq_size
    me = lax.axis_index("fsdp") * seq_size + lax.axis_index("seq")

    def where(peer):
        return (peer // seq_size, peer % seq_size)

    barrier = pltpu.get_barrier_semaphore()

    def greet(step, carry):
        pl.semaphore_signal(
            barrier, inc=1, device_id=where((me + step) % count), device_id_type=MESH
        )
        return carry

    lax.fori_loop(1, count, greet, 0)
    own = pltpu.make_async_copy(x_ref.at[me], y_ref.at[me], local_sem)
    own.start()
    pl.semaphore_wait(barrier, count - 1)

    def copy_to(peer, source):
        return pltpu.make_async_remote_copy(
            src_ref=x_ref.at[peer],
            dst_ref=y_ref.at[source],
            send_sem=send_sem.at[peer],
            recv_sem=recv_sem.at[source],
            device_id=where(peer),
            device_id_type=MESH,
        )

    def send(step, carry):
        copy_to((me + step) % count, me).start()
        return carry

    def finish(step, carry):
        peer = (me + step) % count
        copy_to(peer, peer).wait()
        return carry

    lax.fori_loop(1, count, send, 0)
    own.wait()
    lax.fori_loop(1, count, finish, 0)


def exchange(blocks, sizes, call_id):
    fsdp_size, seq_size = sizes
    count = fsdp_size * seq_size
    vmem = pl.BlockSpec(memory_space=pltpu.VMEM)
    return pl.pallas_call(
        functools.partial(exchange_kernel, fsdp_size, seq_size),
        out_shape=jax.ShapeDtypeStruct(blocks.shape, blocks.dtype),
        in_specs=[vmem],
        out_specs=vmem,
        scratch_shapes=[
            pltpu.SemaphoreType.DMA((count,)),
            pltpu.SemaphoreType.DMA((count,)),
            pltpu.SemaphoreType.DMA,
        ],
        compiler_params=pltpu.CompilerParams(
            collective_id=call_id, has_side_effects=True, vmem_limit_bytes=40 * 1024 * 1024
        ),
    )(blocks)


def norm_rows(values):
    centred = values - jnp.mean(values, -1, keepdims=True)
    inverse = lax.rsqrt(jnp.mean(centred * centred, -1, keepdims=True) + EPS)
    return (centred * inverse, inverse)


def norm_back(normed, inverse, grad_in):
    return inverse * (
        grad_in
        - jnp.mean(grad_in, -1, keepdims=True)
        - normed * jnp.mean(grad_in * normed, -1, keepdims=True)
    )


def gelu_tanh(values):
    return jax.nn.gelu(values, approximate=True)


def mm(spec, left, right):
    return jnp.einsum(spec, left, right, preferred_element_type=jnp.float32)


def split_heads(rows):
    return rows.reshape(rows.shape[0], rows.shape[1], HEADS, rows.shape[2] // HEADS)


def gather_tokens(rows, whole):
    return rows if whole else lax.all_gather(rows, "seq", axis=1, tiled=True)


def layer_forward(stream, pieces, weights, whole):
    w_qkv, w_out, w_up, w_down = weights
    width = stream.shape[-1]
    normed, inverse = norm_rows(stream)
    hidden_in = (normed * (1.0 + pieces[1]) + pieces[0]).astype(jnp.bfloat16)
    qkv = mm("btd,ed->bte", hidden_in, w_qkv).astype(jnp.bfloat16)
    query_heads = split_heads(qkv[..., :width])
    key_heads = split_heads(gather_tokens(qkv[..., width : 2 * width], whole))
    value_heads = split_heads(gather_tokens(qkv[..., 2 * width :], whole))
    scores = mm("bqhd,bkhd->bhqk", query_heads, key_heads) * (width // HEADS) ** (-0.5)
    exp_scores = jnp.exp(scores - jnp.max(scores, -1, keepdims=True))
    soft_full = exp_scores / jnp.sum(exp_scores, -1, keepdims=True)
    soft_probs = soft_full.astype(jnp.bfloat16)
    mixed = mm("bhqk,bkhd->bqhd", soft_probs, value_heads).reshape(stream.shape)
    mixed = mixed.astype(jnp.bfloat16)
    branch = mm("btd,ed->bte", mixed, w_out)
    middle = stream + pieces[2] * branch
    normed_mlp, inverse_mlp = norm_rows(middle)
    hidden_mlp = (normed_mlp * (1.0 + pieces[4]) + pieces[3]).astype(jnp.bfloat16)
    upper = mm("btd,fd->btf", hidden_mlp, w_up)
    active = gelu_tanh(upper).astype(jnp.bfloat16)
    down = mm("btf,fd->btd", active, w_down)
    saved = (
        normed,
        inverse,
        hidden_in,
        query_heads,
        key_heads,
        value_heads,
        soft_full,
        mixed,
        branch,
        normed_mlp,
        inverse_mlp,
        hidden_mlp,
        upper,
        active,
        down,
    )
    return (middle + pieces[5] * down, saved)


def layer_backward(saved, pieces, weights, grad_out, whole):
    w_qkv, w_out, w_up, w_down = weights
    (
        normed,
        inverse,
        hidden_in,
        query_heads,
        key_heads,
        value_heads,
        soft_full,
        mixed,
        branch,
        normed_mlp,
        inverse_mlp,
        hidden_mlp,
        upper,
        active,
        down,
    ) = saved
    width = grad_out.shape[-1]
    scale_factor = (width // HEADS) ** (-0.5)
    grad_gate_mlp = jnp.sum(grad_out * down, 1)
    grad_down = (pieces[5] * grad_out).astype(jnp.bfloat16)
    weight_down = mm("btf,btd->fd", active, grad_down).astype(jnp.bfloat16)
    grad_active = mm("btd,fd->btf", grad_down, w_down)
    _, gelu_pull = jax.vjp(gelu_tanh, upper)
    grad_upper = gelu_pull(grad_active)[0].astype(jnp.bfloat16)
    weight_up = mm("btf,btd->fd", grad_upper, hidden_mlp).astype(jnp.bfloat16)
    grad_hidden_mlp = mm("btf,fd->btd", grad_upper, w_up)
    grad_shift_mlp = jnp.sum(grad_hidden_mlp, 1)
    grad_scale_mlp = jnp.sum(grad_hidden_mlp * normed_mlp, 1)
    grad_middle = grad_out + norm_back(normed_mlp, inverse_mlp, grad_hidden_mlp * (1.0 + pieces[4]))
    grad_gate_attn = jnp.sum(grad_middle * branch, 1)
    grad_branch = (pieces[2] * grad_middle).astype(jnp.bfloat16)
    weight_out = mm("bte,btd->ed", grad_branch, mixed).astype(jnp.bfloat16)
    grad_mixed = split_heads(mm("bte,ed->btd", grad_branch, w_out).astype(jnp.bfloat16))
    soft_probs = soft_full.astype(jnp.bfloat16)
    grad_probs = mm("bqhd,bkhd->bhqk", grad_mixed, value_heads)
    grad_values = mm("bhqk,bqhd->bkhd", soft_probs, grad_mixed)
    inner = jnp.sum(grad_probs * soft_full, -1, keepdims=True)
    grad_scores = (soft_full * (grad_probs - inner)).astype(jnp.bfloat16)
    grad_queries = mm("bhqk,bkhd->bqhd", grad_scores, key_heads) * scale_factor
    grad_keys = mm("bhqk,bqhd->bkhd", grad_scores, query_heads) * scale_factor
    rows = grad_out.shape[:2]
    grad_queries = grad_queries.reshape(grad_out.shape).astype(jnp.bfloat16)
    grad_keys = grad_keys.reshape(rows[0], -1, width).astype(jnp.bfloat16)
    grad_values = grad_values.reshape(rows[0], -1, width).astype(jnp.bfloat16)
    if not whole:
        grad_keys = lax.psum_scatter(grad_keys, "seq", scatter_dimension=1, tiled=True)
        grad_values = lax.psum_scatter(grad_values, "seq", scatter_dimension=1, tiled=True)
    grad_qkv = jnp.concatenate([grad_queries, grad_keys, grad_values], -1)
    weight_qkv = mm("bte,btd->ed", grad_qkv, hidden_in).astype(jnp.bfloat16)
    grad_hidden = mm("bte,ed->btd", grad_qkv, w_qkv)
    grad_shift_attn = jnp.sum(grad_hidden, 1)
    grad_scale_attn = jnp.sum(grad_hidden * normed, 1)
    grad_stream = grad_middle + norm_back(normed, inverse, grad_hidden * (1.0 + pieces[1]))
    grad_mod = jnp.concatenate(
        [
            grad_shift_attn,
            grad_scale_attn,
            grad_gate_attn,
            grad_shift_mlp,
            grad_scale_mlp,
            grad_gate_mlp,
        ],
        -1,
    )
    return (grad_stream, (weight_qkv, weight_out, weight_up, weight_down), grad_mod)


def swap_tokens(values, seq_size):
    me = lax.axis_index("seq")
    keep = lax.dynamic_index_in_dim(values, me, 0, keepdims=False)
    give = lax.dynamic_index_in_dim(values, 1 - me, 0, keepdims=False)
    other = lax.ppermute(give, "seq", [(0, 1), (1, 0)])
    return jnp.concatenate([keep, other], 0)[None]


def swap_back(values, seq_size):
    me = lax.axis_index("seq")
    tokens = values.shape[1] // 2
    keep, give = values[0, :tokens], values[0, tokens:]
    other = lax.ppermute(give, "seq", [(0, 1), (1, 0)])
    first = jnp.where(me == 0, keep, other)
    second = jnp.where(me == 0, other, keep)
    return jnp.stack([first, second])


def local(sizes, latents, cond_pick, cond_table, w_ada, b_ada, w_qkv, w_out, w_up, w_down, cotangent):
    fsdp_size, seq_size = sizes
    count = fsdp_size * seq_size
    layers, width, ada_cols = w_ada.shape
    local_latents = latents.shape[0]
    all_latents = local_latents * fsdp_size
    whole = seq_size == 2 and local_latents == 2
    fsdp_me = lax.axis_index("fsdp")
    seq_me = lax.axis_index("seq")

    parts = [w_qkv.shape[2], w_out.shape[2], w_up.shape[2], w_down.shape[1]]
    starts = [sum(parts[:index]) for index in range(5)]
    gathered = []
    for layer in range(layers):
        packed = jnp.concatenate(
            [w_qkv[layer].T, w_out[layer].T, w_up[layer].T, w_down[layer]], 0
        )
        gathered.append(lax.all_gather(packed, BOTH, axis=0, tiled=False))

    def unpack(block):
        return tuple(
            block[:, starts[index] : starts[index + 1]].reshape(-1, width) for index in range(4)
        )

    pick_rows = jnp.broadcast_to(
        jnp.pad(cond_pick.astype(jnp.float32), (0, 128 - local_latents))[None, None],
        (count, 8, 128),
    )
    picks = exchange(pick_rows, sizes, 0)[::seq_size, 0, :local_latents].reshape(-1)
    picks = picks.astype(jnp.int32)
    table_rows = cond_table.shape[0]
    one_hot = (picks[:, None] == jnp.arange(table_rows, dtype=jnp.int32)[None, :]).astype(
        jnp.float32
    )
    condition_all = jnp.dot(one_hot, cond_table, precision=HIGH, preferred_element_type=jnp.float32)
    silu_all = jax.nn.silu(condition_all)
    mod_cols = jnp.stack(
        [
            jnp.dot(
                silu_all,
                w_ada[layer].astype(jnp.float32),
                precision=HIGH,
                preferred_element_type=jnp.float32,
            )
            + b_ada[layer].astype(jnp.float32)
            for layer in range(layers)
        ]
    )
    mod_send = mod_cols.reshape(layers, fsdp_size, 1, local_latents, ada_cols)
    mod_send = jnp.broadcast_to(
        mod_send.transpose(1, 2, 0, 3, 4),
        (fsdp_size, seq_size, layers, local_latents, ada_cols),
    ).reshape(count, layers * local_latents, ada_cols)
    mod_mine = (
        exchange(mod_send, sizes, 1)
        .reshape(count, layers, local_latents, ada_cols)
        .transpose(1, 2, 0, 3)
        .reshape(layers, local_latents, 6, width)
    )
    if whole:
        mod_mine = lax.dynamic_slice_in_dim(mod_mine, seq_me, 1, 1)

    stream = swap_tokens(latents, seq_size) if whole else latents
    grad_stream = swap_tokens(cotangent, seq_size) if whole else cotangent
    weights_of, pieces_of, saved_of = [], [], []
    for layer in range(layers):
        weights_of.append(unpack(gathered[layer]))
        pieces_of.append([mod_mine[layer, :, None, piece] for piece in range(6)])
        stream, saved = layer_forward(stream, pieces_of[layer], weights_of[layer], whole)
        saved_of.append(saved)
    output = swap_back(stream, seq_size) if whole else stream

    summed = [None] * layers
    mod_grads = [None] * layers
    for layer in reversed(range(layers)):
        grad_stream, grads, mod_grads[layer] = layer_backward(
            saved_of[layer], pieces_of[layer], weights_of[layer], grad_stream, whole
        )
        packed = jnp.concatenate([grad.reshape(count, -1, width) for grad in grads], 1)
        summed[layer] = lax.psum_scatter(packed, BOTH, scatter_dimension=0, tiled=False)
    grad_latents = swap_back(grad_stream, seq_size) if whole else grad_stream

    grad_mod = jnp.stack(mod_grads)
    rows = grad_mod.shape[1]
    mod_send = (
        grad_mod.reshape(layers, rows, count, ada_cols)
        .transpose(2, 0, 1, 3)
        .reshape(count, layers * rows, ada_cols)
    )
    mod_all = exchange(mod_send, sizes, 2).reshape(fsdp_size, seq_size, layers, rows, ada_cols)
    if whole:
        mod_all = mod_all.transpose(2, 0, 1, 3, 4)
    else:
        mod_all = jnp.sum(mod_all, 1).transpose(1, 0, 2, 3)
    mod_all = mod_all.reshape(layers, all_latents, ada_cols)
    grad_w_ada = jnp.stack(
        [
            jnp.dot(
                silu_all.T, mod_all[layer], precision=HIGH, preferred_element_type=jnp.float32
            )
            for layer in range(layers)
        ]
    )
    grad_b_ada = jnp.sum(mod_all, 1)
    grad_cond = sum(
        jnp.einsum(
            "be,de->bd",
            mod_all[layer],
            w_ada[layer].astype(jnp.float32),
            precision=HIGH,
            preferred_element_type=jnp.float32,
        )
        for layer in range(layers)
    )
    table_cols = width // count
    cond_send = grad_cond.reshape(all_latents, count, table_cols).transpose(1, 0, 2)
    grad_cond_cols = jnp.sum(exchange(cond_send, sizes, 3), 0)
    me = fsdp_me * seq_size + seq_me
    cond_cols = lax.dynamic_slice_in_dim(condition_all, me * table_cols, table_cols, 1)
    _, silu_pull = jax.vjp(jax.nn.silu, cond_cols)
    grad_table = jnp.dot(
        one_hot.T,
        silu_pull(grad_cond_cols)[0],
        precision=HIGH,
        preferred_element_type=jnp.float32,
    )

    stacked = jnp.stack(summed).astype(jnp.float32)
    grads = [stacked[:, starts[index] : starts[index + 1]] for index in range(4)]
    return (
        output,
        grad_latents,
        grad_table,
        grad_w_ada,
        grad_b_ada,
        jnp.swapaxes(grads[0], 1, 2),
        jnp.swapaxes(grads[1], 1, 2),
        jnp.swapaxes(grads[2], 1, 2),
        grads[3],
    )


def solution(mesh):
    sizes = (mesh.shape["fsdp"], mesh.shape["seq"])
    columns = P(None, None, BOTH)
    tokens = P("fsdp", "seq", None)
    return jax.shard_map(
        functools.partial(local, sizes),
        mesh=mesh,
        in_specs=(
            tokens,
            P("fsdp"),
            P(),
            columns,
            P(None, BOTH),
            columns,
            columns,
            columns,
            P(None, BOTH, None),
            tokens,
        ),
        out_specs=(
            tokens,
            tokens,
            P(None, BOTH),
            columns,
            P(None, BOTH),
            columns,
            columns,
            columns,
            P(None, BOTH, None),
        ),
        check_vma=False,
    )
```

time: 2300 us -> 653 us (0.28)
  waiting for transfers between devices: 1760 us -> 445 us
  matrix products: 212 us -> 66.3 us
  local copies, waits for them, and re-layouts: 144 us -> 51.7 us
  blocking collectives: 88 us -> 0 us
  other arithmetic: 67.5 us -> 22 us
  Pallas kernels: 0 us -> 43.8 us
    unnamed x36 -> x4, waiting for transfers between devices: 891 us -> 0.07 us
    all_gather x10 -> x2, waiting for transfers between devices: 497 us -> 166 us  [local(): gathered.append(lax.all_gather(packed, BOTH, axis=0, tiled=False))]
    dot_general x81 -> x41, matrix products: 210 us -> 62.5 us  [the longest x34 59.3 us: mm(): return jnp.einsum(spec, left, right, preferred_element_type=jnp.float32)]
    reduce_scatter x2, waiting for transfers between devices: 374 us -> 279 us  [local(): lax.psum_scatter(packed, BOTH, scatter_dimension=0, tiled=False)]
    another operation x12 -> x4, local copies, waits for them, and re-layouts: 89.2 us -> 0.28 us  [the longest x2 0.23 us: local(): grad_mod = jnp.stack(mod_grads)]
    all_gather x8 -> x0, blocking collectives: 45 us -> none  [the longest x4 22.8 us: layer_forward(): lax.all_gather(qkv_rows[..., 2 * model_width:], 'seq', axis=1, tiled=True)]
    another operation x7 -> x5, other arithmetic: 47.5 us -> 3.5 us  [the longest x4 2.53 us: swap_back(): return jnp.stack([first, second])]
    pallas_call x0 -> x4, Pallas kernels: none -> 43.8 us  [exchange(): pl.pallas_call(functools.partial(exchange_kernel, fsdp_size, seq_size), o...]
  transfers between devices with their start and end apart: 24 -> 8, of which waited for: 20 -> 4; matrix products, arithmetic and copies ran while one was open for 14% -> 13% of each run, Pallas kernels for 0% -> 7%
where the time goes in v1:
time: 653 us; the launch traced here: 650 us
  waiting for transfers between devices  445 us (68%)
  matrix products  66.3 us (10%)
  local copies, waits for them, and re-layouts  51.7 us (8%)
  Pallas kernels  43.8 us (7%)
  other arithmetic  22 us (3%)
  between operations  15.7 us (2%)
    reduce_scatter x2, waiting for transfers between devices, local(): lax.psum_scatter(packed, BOTH, scatter_dimension=0, tiled=False)  279 us
    all_gather x2, waiting for transfers between devices, local(): gathered.append(lax.all_gather(packed, BOTH, axis=0, tiled=False))  166 us
    dot_general x34, matrix products, mm(): return jnp.einsum(spec, left, right, preferred_element_type=jnp.float32)  59.3 us
    pallas_call x4, Pallas kernels, exchange(): pl.pallas_call(functools.partial(exchange_kernel, fsdp_size, seq_size), o...  43.8 us
    slice x6, local copies, waits for them, and re-layouts, unpack(): block[:, starts[index]:starts[index + 1]].reshape(-1, width)  28.5 us
  transfers between devices with their start and end apart: 8, of which 4 were waited for; matrix products, arithmetic and copies ran while one was open for 13% of the time, Pallas kernels for 7%

profile of v1, /device:TPU:0, one launch (start us, length us, event | category | flops | bytes accessed | tf_op | source)
XLA Modules:
  0.0 650.0 jit_solution(5484690519990841709)
XLA Ops:
  7.2 0.9 slice_bitcast_fusion.12
  8.2 1.0 slice_bitcast_fusion.10
  9.2 1.0 slice_bitcast_fusion.7
  10.2 1.0 slice_bitcast_fusion.6
  12.1 0.8 pad_maximum_fusion.4
  12.9 1.7 constant_dynamic-slice_fusion.12
  14.7 3.0 collective-permute-start
  17.6 1.8 dynamic-slice_bitcast_fusion.1
  19.5 12.2 %shard_map.169 = f32[32,8,128]{2,1,0:T(8,128)S(1)} custom-call(f32[32,8,128]{2,1,0:T(8,128)S(1)} %broadcast_in_dim.6.x_ref), custom_call_target="tpu_custom_call" | custom-call | tf_op jit(solution)/shard_map/pallas_call | solution.py:65
  31.9 1.2 fusion.44
  34.4 10.6 %shard_map.170 = f32[32,4,144]{2,1,0:T(4,128)S(1)} custom-call(f32[32,4,144]{2,1,0:T(4,128)S(1)} %reshape.934.x_ref), custom_call_target="tpu_custom_call" | custom-call | tf_op jit(solution)/shard_map/pallas_call | solution.py:65
  45.6 75.2 %all-gather.5.cloned.1.call-done = bf16[9216,768]{1,0:T(8,128)(2,1)} async-done(((bf16[288,768]{1,0:T(8,128)(2,1)}), bf16[9216,768]{1,0:T(8,128)(2,1)}) %all-gather.5.cloned.1.call-update) | async-done | bytes 14155792 | tf_op jit(solution)/shard_map/all_gather | solution.py:258
  120.8 1.4 slice.206
  122.1 4.4 slice.202
  126.6 8.2 %fusion.97 = (bf16[32,96,768]{2,1,0:T(8,128)(2,1)}, bf16[32,96,768]{2,1,0:T(8,128)(2,1)}) fusion(bf16[32,288,768]{2,1,0:T(8,128)(2,1)} %bitcast.267), kind=kLoop, calls=%fused_computation.262 | loop fusion | bytes 18874368 | tf_op jit(solution)/shard_map/slice | solution.py:262
  134.8 90.9 %all-gather.7.cloned.1.call-done = bf16[9216,768]{1,0:T(8,128)(2,1)} async-done(((bf16[288,768]{1,0:T(8,128)(2,1)}), bf16[9216,768]{1,0:T(8,128)(2,1)}) %all-gather.7.cloned.1.call-update) | async-done | bytes 14155792 | tf_op jit(solution)/shard_map/all_gather | solution.py:258
  225.7 2.4 slice.213
  228.0 4.1 slice.209
  232.1 8.1 %fusion.96 = (bf16[32,96,768]{2,1,0:T(8,128)(2,1)}, bf16[32,96,768]{2,1,0:T(8,128)(2,1)}) fusion(bf16[32,288,768]{2,1,0:T(8,128)(2,1)} %bitcast.270), kind=kLoop, calls=%fused_computation.261 | loop fusion | bytes 18874368 | tf_op jit(solution)/shard_map/slice | solution.py:262
  240.2 1.3 fusion.2
  242.0 1.3 fusion.101
  244.0 1.3 fusion.95
  245.5 4.0 fusion.89
  249.5 4.7 fusion.94
  254.5 1.3 fusion.3
  256.4 1.3 fusion.102
  259.8 4.1 fusion.90
  264.0 4.6 fusion.17
  268.7 0.9 multiply_reduce_fusion.3
  269.7 3.0 multiply_reduce_fusion.4
  273.7 0.8 copy.54
  274.6 2.5 convolution_convert_fusion.12
  277.0 1.7 multiply_reduce_fusion.1
  279.5 1.3 copy-done.3
  280.8 0.8 multiply_reduce_fusion.5
  282.1 1.0 copy-done.6
  283.1 4.6 fusion.10
  287.8 0.9 multiply_reduce_fusion.7
  290.1 1.0 convolution_convert_fusion.11
  291.1 1.7 copy.58
  292.8 2.4 convolution_convert_fusion.10
  295.3 1.7 multiply_reduce_fusion
  299.5 1.7 convolution_convert_fusion.3
  301.2 1.7 convolution_convert_fusion.4
  303.0 1.2 convolution_convert_fusion.5
  304.2 6.1 pad_maximum_fusion
  310.4 0.9 copy-done.21
  311.3 1.5 convolution_convert_fusion.8
  312.8 1.2 convolution_convert_fusion.2
  314.0 1.5 convolution_convert_fusion.1
  315.5 2.6 convolution_convert_fusion
  318.2 6.1 pad_maximum_fusion.1
  324.3 1.0 copy-done.54
  325.3 1.5 collective-permute-start.1
  327.1 3.1 multiply_reduce_fusion.9
  330.6 8.5 %shard_map.171 = f32[32,2,144]{2,1,0:T(2,128)S(1)} custom-call(f32[32,2,144]{2,1,0:T(2,128)S(1)} %maximum_bitcast_fusion.7.x_ref), custom_call_target="tpu_custom_call" | custom-call | tf_op jit(solution)/shard_map/pallas_call | solution.py:65
  341.4 12.5 %shard_map.172 = f32[32,32,24]{2,1,0:T(8,128)S(1)} custom-call(f32[32,32,24]{2,1,0:T(8,128)S(1)} %bitcast.245), custom_call_target="tpu_custom_call" | custom-call | tf_op jit(solution)/shard_map/pallas_call | solution.py:65
  355.6 1.0 pad_maximum_fusion.2
  356.6 1.0 fusion.43
  357.6 1.0 select_bitcast_fusion.3
  360.1 111.4 %reduce-scatter.3.cloned.1.call-done = bf16[1,288,768]{2,1,0:T(8,128)(2,1)} async-done(((bf16[32,288,768]{2,1,0:T(8,128)(2,1)}), bf16[1,288,768]{2,1,0:T(8,128)(2,1)}) %reduce-scatter.3.cloned.1.call-update) | async-done | bytes 442384 | tf_op jit(solution)/shard_map/reduce_scatter | solution.py:320
  471.6 167.5 %reduce-scatter.5.cloned.1.call-done = bf16[1,288,768]{2,1,0:T(8,128)(2,1)} async-done(((bf16[32,288,768]{2,1,0:T(8,128)(2,1)}), bf16[1,288,768]{2,1,0:T(8,128)(2,1)}) %reduce-scatter.5.cloned.1.call-update) | async-done | bytes 442384 | tf_op jit(solution)/shard_map/reduce_scatter | solution.py:320
  639.0 1.3 maximum_convert_fusion
  641.1 1.1 fusion.98
  (246 shorter events, 20.9 us)
Async XLA Ops:
  7.2 24.7 %copy-start = (f32[1000,768]{1,0:T(8,128)S(1)}, f32[1000,768]{1,0:T(8,128)}, u32[]{:S(2)}) copy-start(f32[1000,768]{1,0:T(8,128)} %param.12) | copy-start | bytes 9216004
  7.2 113.6 %all-gather.5.cloned.1.call-start = ((), (), s32[]{:S(2)}) async-start(), calls=%async_computation.4 | async-start | bytes 14598144 | tf_op jit(solution)/shard_map/all_gather | solution.py:258
  12.0 7.4 %copy-start.62 = (s32[2]{0:T(128)S(1)}, s32[2]{0:T(128)}, u32[]{:S(2)}) copy-start(s32[2]{0:T(128)} %param.11) | copy-start | bytes 28
  12.0 213.7 %all-gather.7.cloned.1.call-start = ((), (), s32[]{:S(2)}) async-start(), calls=%async_computation.5 | async-start | bytes 14598144 | tf_op jit(solution)/shard_map/all_gather | solution.py:258
  12.0 19.8 %copy-start.61 = (bf16[2,144]{1,0:T(2,128)(2,1)S(1)}, bf16[2,144]{1,0:T(2,128)(2,1)}, u32[]{:S(2)}) copy-start(bf16[2,144]{1,0:T(2,128)(2,1)} %param.14) | copy-start | bytes 1732
  12.9 458.7 %reduce-scatter.3.cloned.1.call-start = ((), (), s32[]{:S(2)}) async-start(), calls=%async_computation.2 | async-start | bytes 14598144 | tf_op jit(solution)/shard_map/reduce_scatter | solution.py:320
  14.7 30.6 %collective-permute-start = (f32[64,768]{1,0:T(8,128)}, f32[64,768]{1,0:T(8,128)S(1)}, u32[]{:S(2)}, u32[]{:S(2)}) collective-permute-start(f32[64,768]{1,0:T(8,128)} %get-tuple-element.72), channel_id=1, source_target_pairs={{0,1},{1,0},{2,3},{3,2},{4,5},{5,4},{6,7},{7,6},{8,9},{9,8},{10,11... | collective-permute-start | bytes 589832 | tf_op jit(solution)/shard_map/ppermute | solution.py:227
  19.4 244.6 %collective-permute-start.2 = (f32[64,768]{1,0:T(8,128)}, f32[64,768]{1,0:T(8,128)}, u32[]{:S(2)}, u32[]{:S(2)}) collective-permute-start(f32[64,768]{1,0:T(8,128)} %get-tuple-element.70), channel_id=1, source_target_pairs={{0,1},{1,0},{2,3},{3,2},{4,5},{5,4},{6,7},{7,6},{8,9},{9,8},{10,11... | collective-permute-start | bytes 589832 | tf_op jit(solution)/shard_map/ppermute | solution.py:227
  122.1 121.9 %copy-start.8 = (bf16[32,24,768]{2,1,0:T(8,128)(2,1)}, bf16[32,24,768]{2,1,0:T(8,128)(2,1)S(1)}, u32[]{:S(2)}) copy-start(bf16[32,24,768]{2,1,0:T(8,128)(2,1)S(1)} %slice.206) | copy-start | bytes 3538948
  232.1 8.1 %copy-start.4 = (bf16[32,72,768]{2,1,0:T(8,128)(2,1)S(1)}, bf16[32,72,768]{2,1,0:T(8,128)(2,1)}, u32[]{:S(2)}) copy-start(bf16[32,72,768]{2,1,0:T(8,128)(2,1)} %slice.202) | copy-start | bytes 10616836
  241.7 2.3 copy-start.40
  241.9 2.1 copy-start.42
  242.0 2.0 copy-start.58
  244.0 1.5 copy-start.35
  249.5 4.8 copy-start.5
  249.5 5.0 copy-start.2
  256.0 2.3 copy-start.44
  256.2 2.1 copy-start.46
  256.4 2.0 copy-start.59
  258.3 5.6 copy-start.37
  259.0 5.0 copy-start.50
  259.8 8.8 %slice-start.2 = ((s8[4718592]{0:T(1024)(128)(4,1)}), s8[4194304]{0:T(1024)(128)(4,1)S(1)}, s32[]{:S(2)}) async-start(s8[4718592]{0:T(1024)(128)(4,1)} %bitcast.252), calls=%async_computation.8 | async-start | bytes 8388608
  259.8 9.8 %slice-start.4 = ((s8[4718592]{0:T(1024)(128)(4,1)}), s8[4194304]{0:T(1024)(128)(4,1)S(1)}, s32[]{:S(2)}) async-start(s8[4718592]{0:T(1024)(128)(4,1)} %bitcast.287), calls=%async_computation.10 | async-start | bytes 8388608
  264.0 4.6 slice-start.3
  264.0 5.6 slice-start.5
  269.7 3.7 copy-start.11
  274.6 2.5 copy-start.60
  277.0 1.7 copy-start.49
  277.0 1.9 copy-start.47
  277.0 2.2 copy-start.45
  277.0 2.5 copy-start.38
  278.7 2.1 copy-start.3
  279.5 2.1 copy-start.24
  281.7 1.5 copy-start.6
  281.9 5.9 slice-start
  282.1 6.7 %copy-start.22 = (f32[128,768]{1,0:T(8,128)}, f32[128,768]{1,0:T(8,128)S(1)}, u32[]{:S(2)}) copy-start(f32[128,768]{1,0:T(8,128)S(1)} %get-tuple-element.40) | copy-start | bytes 1179652
  283.1 4.7 slice-start.1
  287.8 1.3 copy-start.28
  288.8 1.3 copy-start.9
  295.3 1.8 copy-start.48
  297.0 1.3 copy-start.41
  297.0 1.5 copy-start.17
  297.0 1.5 copy-start.36
  297.9 1.5 copy-start.7
  297.9 1.6 copy-start.23
  298.3 4.7 copy-start.31
  298.6 4.4 copy-start.33
  299.5 1.7 copy-start.15
  301.2 1.8 copy-start.56
  310.3 328.7 %reduce-scatter.5.cloned.1.call-start = ((), (), s32[]{:S(2)}) async-start(), calls=%async_computation.3 | async-start | bytes 14598144 | tf_op jit(solution)/shard_map/reduce_scatter | solution.py:320
  311.3 1.5 copy-start.25
  311.3 1.5 copy-start.39
  314.0 1.5 copy-start.51
  324.2 2.8 copy-start.32
  324.2 2.8 copy-start.34
  324.2 2.8 copy-start.57
  325.3 32.3 %collective-permute-start.1 = (f32[64,768]{1,0:T(8,128)S(1)}, f32[64,768]{1,0:T(8,128)}, u32[]{:S(2)}, u32[]{:S(2)}) collective-permute-start(f32[64,768]{1,0:T(8,128)S(1)} %slice_bitcast_fusion.4), channel_id=1, source_target_pairs={{0,1},{1,0},{2,3},{3,2},{4,5},{5,4},{6,7},{7,6},{8,9},{9,8},{10,11... | collective-permute-start | bytes 589832 | tf_op jit(solution)/shard_map/ppermute | solution.py:235
  327.1 12.3 %copy-start.18 = (f32[128,768]{1,0:T(8,128)S(1)}, f32[128,768]{1,0:T(8,128)}, u32[]{:S(2)}) copy-start(f32[128,768]{1,0:T(8,128)} %copy-done.16) | copy-start | bytes 1179652
  330.2 10.0 %copy-start.53 = (bf16[2,768,144]{1,2,0:T(8,128)(2,1)S(1)}, bf16[2,768,144]{1,2,0:T(8,128)(2,1)}, u32[]{:S(2)}) copy-start(bf16[2,768,144]{1,2,0:T(8,128)(2,1)} %param.13) | copy-start | bytes 1327108
  339.6 19.8 %collective-permute-start.3 = (f32[64,768]{1,0:T(8,128)S(1)}, f32[64,768]{1,0:T(8,128)S(1)}, u32[]{:S(2)}, u32[]{:S(2)}) collective-permute-start(f32[64,768]{1,0:T(8,128)S(1)} %slice_bitcast_fusion.2), channel_id=1, source_target_pairs={{0,1},{1,0},{2,3},{3,2},{4,5},{5,4},{6,7},{7,6},{8,9},{9,8},{10,11... | collective-permute-start | bytes 589832 | tf_op jit(solution)/shard_map/ppermute | solution.py:235
  340.7 13.8 %copy-start.30 = (f32[32,768]{1,0:T(8,128)S(1)}, f32[32,768]{1,0:T(8,128)}, u32[]{:S(2)}) copy-start(f32[32,768]{1,0:T(8,128)} %copy-done.29) | copy-start | bytes 294916
  640.3 1.9 copy-start.26
  640.3 1.9 copy-start.27
  640.3 2.7 copy-start.1
  (13 other events, 12.8 us)
Sparse Core Ops, SparseCore 0:
  12.1 108.6 all-gather.4
  124.3 101.3 all-gather.6
  310.5 161.0 reduce-scatter.2
  477.4 161.5 reduce-scatter.4
